TPU v7x, 512 devices: a whole 4x8x8 slice. The times are simulated.
512 devices in a mesh: pipe: 4 (over x), ctx: 16 (over z, core), tp: 8 (over y).
Axes of the slice: x: 4, y: 8, z: 8, core: 2. Of those that a mesh axis runs over, the one named last changes fastest.
Arguments:
- values: bfloat16 [4, 4096, 8192], P('pipe', 'ctx', 'tp'), may hold values from -6 to 6
- gates: bfloat16 [4, 4096, 8192], P('pipe', 'ctx', 'tp'), may hold values from -6 to 6
- incoming: bfloat16 [4, 4096, 8192], P('pipe', 'ctx', 'tp'), may hold values from -6 to 6
- filters: bfloat16 [4, 512, 128], P('pipe', 'tp'), may hold values from -0.5 to 0.5
- doc_lengths: int32 [16], replicated, may hold values from 1 to 384, 4096 in all
Outputs:
- value_grad: bfloat16 [4, 4096, 8192], P('pipe', 'ctx', 'tp')
- gate_grad: bfloat16 [4, 4096, 8192], P('pipe', 'ctx', 'tp')
- filter_grad: float32 [4, 512, 128], P('pipe', 'tp')
All inputs are finite; a program needn't handle non-finite values.
Results may differ from a plain program's by a relative error of at most 0.0049.
Values may be sent and summed in bfloat16 or wider, within the bound.
A program may use at most 64 MiB of HBM per device.

v0:
```python
import jax
import jax.numpy as jnp
from jax import lax
from jax.sharding import PartitionSpec as P

BLOCK = 128


def shifted(block, axis, distance):
    devices = range(lax.axis_size(axis))
    route = [((i - distance) % len(devices), i) for i in devices]
    return lax.ppermute(block, axis, route)


def shifted_2(value, axis, by):
    length = lax.axis_size(axis)
    pairs = [(i, i + by) for i in range(length) if 0 <= i + by < length]
    return lax.ppermute(value, axis, pairs)


def owners(positions, starts):
    before = starts[None, :] <= positions[:, None]
    return jnp.max(jnp.where(before, starts[None, :], 0), axis=1)


def skew_table(pattern, nout, win):
    groups, taps = pattern.shape
    period = win + 1
    padded = jnp.concatenate([pattern, jnp.zeros((groups, period - taps), pattern.dtype)], axis=1)
    tiled = jnp.tile(padded, (1, nout))[:, : nout * win]
    return tiled.reshape(groups, nout, win)


def down_mask(begin, blk, win, starts):
    rim = win - blk
    here = begin + jnp.arange(blk, dtype=jnp.int32)
    source = begin - rim + jnp.arange(win, dtype=jnp.int32)
    return source[None, :] >= owners(here, starts)[:, None]


def up_mask(begin, nout, win, starts):
    target = begin + jnp.arange(nout, dtype=jnp.int32)
    source = begin + jnp.arange(win, dtype=jnp.int32)
    return target[:, None] >= owners(source, starts)[None, :]


def forward_conv(extended, table, starts, first, rows):
    groups, blk, win = table.shape

    def forward_one(index):
        window = lax.dynamic_slice_in_dim(extended, index * blk, win, 0)
        mask = down_mask(first + index * blk, blk, win, starts).astype(table.dtype)
        weights = table * mask[None]
        return jnp.einsum("gij,jgc->igc", weights, window, preferred_element_type=jnp.float32)

    out = lax.map(forward_one, jnp.arange(rows // blk, dtype=jnp.int32))
    return out.reshape(rows, -1)


def upward(grad_window, table, starts, begin):
    groups, nout, win = table.shape
    mask = up_mask(begin, nout, win, starts).astype(table.dtype)
    weights = table * mask[None]
    return jnp.einsum("gij,jgc->igc", weights, grad_window, preferred_element_type=jnp.float32)


def transpose_conv(grad_rows, table, starts, first, rows):
    groups, blk, win = table.shape

    def transpose_one(index):
        window = lax.dynamic_slice_in_dim(grad_rows, index * blk, win, 0)
        return upward(window, table, starts, first + index * blk)

    out = lax.map(transpose_one, jnp.arange(rows // blk, dtype=jnp.int32))
    return out.reshape(rows, -1)


def lag_sums(product, blk, win, taps):
    groups = product.shape[0]
    flat = product.reshape(groups, blk * win)
    flat = jnp.concatenate([flat, jnp.zeros((groups, blk), jnp.float32)], axis=1)
    skewed = flat.reshape(groups, blk, win + 1)[:, :, :taps]
    return jnp.flip(jnp.sum(skewed, axis=1), axis=1)


def filter_terms(grad_rows, extended, starts, first, rows, blk, taps):
    groups = grad_rows.shape[1]
    win = blk + taps - 1

    def step(index, total):
        part = lax.dynamic_slice_in_dim(grad_rows, index * blk, blk, 0)
        window = lax.dynamic_slice_in_dim(extended, index * blk, win, 0)
        mask = down_mask(first + index * blk, blk, win, starts)
        product = jnp.einsum("igc,jgc->gij", part, window, preferred_element_type=jnp.float32)
        product = jnp.where(mask[None], product, jnp.zeros_like(product))
        return total + lag_sums(product, blk, win, taps)

    return lax.fori_loop(0, rows // blk, step, jnp.zeros((groups, taps), jnp.float32))


def body(values, gates, incoming, filters, doc_lengths):
    current = values[0]
    gate_vals = gates[0]
    filt = filters[0]
    rows, width = current.shape
    groups, taps = filt.shape
    chans = width // groups
    rim = taps - 1
    win = BLOCK + rim
    first = lax.axis_index("ctx") * rows
    starts = jnp.cumsum(doc_lengths) - doc_lengths
    out_grad = shifted(incoming, "pipe", -1)[0]
    earlier = shifted_2(current[rows - rim :], "ctx", 1)
    extended = jnp.concatenate([earlier, current], axis=0).reshape(rows + rim, groups, chans)
    table = skew_table(jnp.flip(filt, axis=1), BLOCK, win)
    conv = forward_conv(extended, table, starts, first, rows)
    gate_grad = (out_grad.astype(jnp.float32) * conv).astype(jnp.bfloat16)
    conv_grad = (out_grad.astype(jnp.float32) * gate_vals.astype(jnp.float32)).astype(jnp.bfloat16)
    grad_rows = conv_grad.reshape(rows, groups, chans)
    partial_filter = filter_terms(grad_rows, extended, starts, first, rows, BLOCK, taps)
    filter_grad = lax.psum(partial_filter, "ctx")
    upper = skew_table(filt, BLOCK, win)
    blank = jnp.zeros((rim, groups, chans), jnp.bfloat16)
    longer = jnp.concatenate([grad_rows, blank], axis=0)
    local = transpose_conv(longer, upper, starts, first, rows)
    edge_window = jnp.concatenate([blank, grad_rows[:rim]], axis=0)
    edge = upward(edge_window, skew_table(filt, rim, 2 * rim), starts, first - rim)
    edge_rows = edge.reshape(rim, width)
    returned = shifted_2(edge_rows, "ctx", -1)
    value_grad = local + jnp.concatenate(
        [jnp.zeros((rows - rim, width), jnp.float32), returned], axis=0
    )
    return (value_grad.astype(jnp.bfloat16)[None], gate_grad[None], filter_grad[None])


def solution(mesh):
    in_specs = (
        P("pipe", "ctx", "tp"),
        P("pipe", "ctx", "tp"),
        P("pipe", "ctx", "tp"),
        P("pipe", "tp", None),
        P(),
    )
    out_specs = (P("pipe", "ctx", "tp"), P("pipe", "ctx", "tp"), P("pipe", "tp", None))
    return jax.shard_map(body, mesh=mesh, in_specs=in_specs, out_specs=out_specs, check_vma=False)
```

profile of v0, /device:TPU:1, one launch (start us, length us, event | category | flops | bytes accessed | tf_op | source)
XLA Modules:
  0.0 261.6 jit_solution(9768795199470018805)
XLA Ops:
  1.7 5.4 %collective-permute-start.2 = (bf16[127,1024]{1,0:T(8,128)(2,1)S(1)}, bf16[127,1024]{1,0:T(8,128)(2,1)S(1)}, u32[]{:S(2)}, u32[]{:S(2)}) collective-permute-start(bf16[127,1024]{1,0:T(8,128)(2,1)S(1)} %slice_bitcast_fusion), channel_id=1, source_target_pairs={{0,8},{8,16},{16,24},{24,32},{32,40},{40,48},{48,56},{56,64},{64,7... | collective-permute-start | bytes 780296 | tf_op jit(solution)/shard_map/ppermute | solution.py:18
  9.1 4.4 %collective-permute-start = (bf16[1,256,1024]{1,2,0:T(8,128)(2,1)}, bf16[1,256,1024]{1,2,0:T(8,128)(2,1)}, u32[]{:S(2)}, u32[]{:S(2)}) collective-permute-start(bf16[1,256,1024]{1,2,0:T(8,128)(2,1)} %copy.26), channel_id=1, source_target_pairs={{128,0},{256,128},{384,256},{0,384},{129,1},{257,129},{385,257},{1... | collective-permute-start | bytes 1572872 | tf_op jit(solution)/shard_map/ppermute | solution.py:12
  23.8 15.9 %reshape.263 = bf16[64,128,255]{2,1,0:T(8,128)(2,1)} reshape(bf16[64,32640]{1,0:T(8,128)(2,1)} %slice.44) | data formatting | bytes 8355840 | tf_op jit(solution)/shard_map/reshape | solution.py:31
  42.9 8.6 %tile.30 = bf16[64,32385]{1,0:T(8,128)(2,1)} reshape(bf16[64,127,255]{2,1,0:T(8,128)(2,1)} %tile.14) | data formatting | bytes 8290560 | tf_op jit(solution)/shard_map/tile | solution.py:30
  51.5 4.4 %slice.43 = bf16[64,32258]{1,0:T(8,128)(2,1)} slice(bf16[64,32385]{1,0:T(8,128)(2,1)} %tile.30), slice={[0:64], [0:32258]} | slice | bytes 8258048 | tf_op jit(solution)/shard_map/slice | solution.py:30
  55.9 16.0 %reshape.261 = bf16[64,127,254]{2,1,0:T(8,128)(2,1)} reshape(bf16[64,32258]{1,0:T(8,128)(2,1)} %slice.43) | data formatting | bytes 8258048 | tf_op jit(solution)/shard_map/reshape | solution.py:31
  77.1 15.8 %reshape.259 = bf16[64,128,255]{2,1,0:T(8,128)(2,1)} reshape(bf16[64,32640]{1,0:T(8,128)(2,1)} %slice.41) | data formatting | bytes 8355840 | tf_op jit(solution)/shard_map/reshape | solution.py:31
  94.1 30.7 %while.39 = (s32[]{:T(128)}, f32[2,128,64,16]{1,0,3,2:T(2,128)S(1)}, s32[2]{0:T(128)S(1)}, bf16[383,64,16]{0,2,1:T(8,128)(2,1)S(1)}, s32[]{:T(128)}, /*index=5*/...) while((s32[]{:T(128)}, ...), condition=%wide.region_7.8_spmd, body=%wide.region_5.7_spmd.sunk | while | flops 69007368 | bytes 6410255 | solution.py:56
  99.0 10.4 %dynamic_update_slice.13 = f32[2,128,64,16]{1,0,3,2:T(2,128)S(1)} dynamic-update-slice(f32[2,128,64,16]{1,0,3,2:T(2,128)S(1)} %get-tuple-element.497, f32[1,128,64,16]{1,0,3,2:T(1,128)S(1)} %bitcast.58, s32[]{:T(128)} %get-tuple-element.496, s32[]{:T(128)} %constant.149.clone.1..sunk.1, s32[]{:T(128)} %constant.149.clone.1..sunk.1, s32[]{:T(128)} %constant.149.clone.1..sunk.1) | dynamic-update-slice | bytes 1048580 | tf_op jit(solution)/shard_map/while/body/jit(dynamic_update_index_in_dim)/dynamic_update_slice | solution.py:56
  111.0 3.4 %fusion.35 = f32[64,16,128]{2,1,0:T(8,128)S(1)} fusion(bf16[64,128,255]{2,1,0:T(8,128)(2,1)} %get-tuple-element.514, bf16[128,255]{1,0:T(8,128)(2,1)S(1)} %compare_convert_fusion.6, bf16[383,64,16]{0,2,1:T(8,128)(2,1)S(1)} %get-tuple-element.511, s32[]{:T(128)S(6)} %select_n.86), kind=kOutput, calls=%fused_computation.9.clone.1 | convolution fusion | flops 68935680 | bytes 5292036 | tf_op jit(solution)/shard_map/while/body/eval_jaxpr/gij,jgc->igc/dot_general | solution.py:54
  114.4 10.4 %dynamic_update_slice.13 = f32[2,128,64,16]{1,0,3,2:T(2,128)S(1)} dynamic-update-slice(f32[2,128,64,16]{1,0,3,2:T(2,128)S(1)} %get-tuple-element.497, f32[1,128,64,16]{1,0,3,2:T(1,128)S(1)} %bitcast.58, s32[]{:T(128)} %get-tuple-element.496, s32[]{:T(128)} %constant.149.clone.1..sunk.1, s32[]{:T(128)} %constant.149.clone.1..sunk.1, s32[]{:T(128)} %constant.149.clone.1..sunk.1) | dynamic-update-slice | bytes 1048580 | tf_op jit(solution)/shard_map/while/body/jit(dynamic_update_index_in_dim)/dynamic_update_slice | solution.py:56
  127.9 4.2 %fusion.13 = f32[64,16,127]{2,1,0:T(8,128)} fusion(bf16[64,127,254]{2,1,0:T(8,128)(2,1)} %reshape.261, bf16[127,254]{1,0:T(8,128)(2,1)S(1)} %compare_convert_fusion.2, bf16[127,64,16]{0,2,1:T(8,128)(2,1)S(1)} %bitcast.69), kind=kOutput, calls=%fused_computation.28 | convolution fusion | flops 68128896 | bytes 4973828 | tf_op jit(solution)/shard_map/gij,jgc->igc/dot_general | solution.py:64
  134.4 42.6 %while.40 = (s32[]{:T(128)}, f32[64,128]{1,0:T(8,128)S(1)}, s32[]{:T(128)}, s32[16]{0:T(128)S(1)}, bf16[256,64,16]{0,2,1:T(8,128)(2,1)S(1)}, /*index=5*/bf16[383...) while((s32[]{:T(128)}, f32[64,128]{1,0:T(8,128)S(1)}, ...), condition=%wide.region_11.12_spmd.clone, body=%wide.region_8.11_spmd.clone.sunk | while | flops 70031496 | bytes 63836336 | solution.py:98
  134.9 4.5 %broadcast_select_fusion.2 = f32[64,128,255]{2,1,0:T(8,128)} fusion(pred[128,255]{1,0:T(8,128)(4,1)S(1)} %broadcast_compare_fusion.2, bf16[383,64,16]{0,2,1:T(8,128)(2,1)S(1)} %get-tuple-element.584, s32[]{:T(128)S(6)} %select_n.89, bf16[256,64,16]{0,2,1:T(8,128)(2,1)S(1)} %get-tuple-element.583, s32[]{:T(128)S(6)} %select_n.90), kind=kOutput, calls=%fused_computation.19.clone.1 | convolution fusion | flops 68935680 | bytes 9175048 | tf_op jit(solution)/shard_map/while/body/eval_jaxpr/igc,jgc->gij/dot_general | solution.py:94
  139.4 9.3 %reshape.269 = f32[64,32640]{1,0:T(8,128)} reshape(f32[64,128,255]{2,1,0:T(8,128)} %broadcast_select_fusion.2) | data formatting | bytes 16711680 | tf_op jit(solution)/shard_map/while/body/eval_jaxpr/reshape | solution.py:80
  148.7 4.0 %concatenate.47 = f32[64,32768]{1,0:T(8,128)S(1)} pad(f32[64,32640]{1,0:T(8,128)} %reshape.269, f32[]{:T(128)} %constant.150.clone.1..sunk), padding=0_0x0_128 | pad | bytes 16744452 | tf_op jit(solution)/shard_map/while/body/eval_jaxpr/concatenate | solution.py:81
  156.1 4.5 %broadcast_select_fusion.2 = f32[64,128,255]{2,1,0:T(8,128)} fusion(pred[128,255]{1,0:T(8,128)(4,1)S(1)} %broadcast_compare_fusion.2, bf16[383,64,16]{0,2,1:T(8,128)(2,1)S(1)} %get-tuple-element.584, s32[]{:T(128)S(6)} %select_n.89, bf16[256,64,16]{0,2,1:T(8,128)(2,1)S(1)} %get-tuple-element.583, s32[]{:T(128)S(6)} %select_n.90), kind=kOutput, calls=%fused_computation.19.clone.1 | convolution fusion | flops 68935680 | bytes 9175048 | tf_op jit(solution)/shard_map/while/body/eval_jaxpr/igc,jgc->gij/dot_general | solution.py:94
  160.6 9.3 %reshape.269 = f32[64,32640]{1,0:T(8,128)} reshape(f32[64,128,255]{2,1,0:T(8,128)} %broadcast_select_fusion.2) | data formatting | bytes 16711680 | tf_op jit(solution)/shard_map/while/body/eval_jaxpr/reshape | solution.py:80
  169.8 4.0 %concatenate.47 = f32[64,32768]{1,0:T(8,128)S(1)} pad(f32[64,32640]{1,0:T(8,128)} %reshape.269, f32[]{:T(128)} %constant.150.clone.1..sunk), padding=0_0x0_128 | pad | bytes 16744452 | tf_op jit(solution)/shard_map/while/body/eval_jaxpr/concatenate | solution.py:81
  177.5 30.8 %while.38 = (s32[]{:T(128)}, f32[2,128,64,16]{1,0,3,2:T(2,128)S(1)}, s32[2]{0:T(128)S(1)}, bf16[383,64,16]{0,2,1:T(8,128)(2,1)S(1)}, s32[]{:T(128)}, /*index=5*/...) while((s32[]{:T(128)}, ...), condition=%wide.region_3.4_spmd, body=%wide.region_1.3_spmd.sunk | while | flops 69013336 | bytes 6411251 | solution.py:74
  182.5 10.4 %dynamic_update_slice.12 = f32[2,128,64,16]{1,0,3,2:T(2,128)S(1)} dynamic-update-slice(f32[2,128,64,16]{1,0,3,2:T(2,128)S(1)} %get-tuple-element.532, f32[1,128,64,16]{1,0,3,2:T(1,128)S(1)} %bitcast.59, s32[]{:T(128)} %get-tuple-element.531, s32[]{:T(128)} %constant.149.clone.1..sunk, s32[]{:T(128)} %constant.149.clone.1..sunk, s32[]{:T(128)} %constant.149.clone.1..sunk) | dynamic-update-slice | bytes 1048580 | tf_op jit(solution)/shard_map/while/body/jit(dynamic_update_index_in_dim)/dynamic_update_slice | solution.py:56
  194.5 3.4 %fusion.32 = f32[64,16,128]{2,1,0:T(8,128)S(1)} fusion(bf16[64,128,255]{2,1,0:T(8,128)(2,1)} %get-tuple-element.548, bf16[128,255]{1,0:T(8,128)(2,1)S(1)} %compare_convert_fusion.5, bf16[383,64,16]{0,2,1:T(8,128)(2,1)S(1)} %get-tuple-element.545, s32[]{:T(128)S(6)} %select_n.84), kind=kOutput, calls=%fused_computation.clone.1 | convolution fusion | flops 68935680 | bytes 5292036 | tf_op jit(solution)/shard_map/while/body/eval_jaxpr/gij,jgc->igc/dot_general | solution.py:64
  198.0 10.4 %dynamic_update_slice.12 = f32[2,128,64,16]{1,0,3,2:T(2,128)S(1)} dynamic-update-slice(f32[2,128,64,16]{1,0,3,2:T(2,128)S(1)} %get-tuple-element.532, f32[1,128,64,16]{1,0,3,2:T(1,128)S(1)} %bitcast.59, s32[]{:T(128)} %get-tuple-element.531, s32[]{:T(128)} %constant.149.clone.1..sunk, s32[]{:T(128)} %constant.149.clone.1..sunk, s32[]{:T(128)} %constant.149.clone.1..sunk) | dynamic-update-slice | bytes 1048580 | tf_op jit(solution)/shard_map/while/body/jit(dynamic_update_index_in_dim)/dynamic_update_slice | solution.py:56
  209.4 49.9 %psum.7 = f32[1,64,128]{2,1,0:T(8,128)} all-reduce(f32[1,64,128]{2,1,0:T(8,128)S(1)} %bitcast.68), channel_id=1, replica_groups=mesh['pipe'=4,'ctx'=16,'tp'=8] {'ctx'}, use_global_device_ids=true, to_apply=%region_12.13 | all-reduce | flops 8192 | bytes 65536 | tf_op jit(solution)/shard_map/psum | solution.py:121
  (83 shorter events, 48.7 us)
Async XLA Ops:
  1.7 91.3 %collective-permute-start.2 = (bf16[127,1024]{1,0:T(8,128)(2,1)S(1)}, bf16[127,1024]{1,0:T(8,128)(2,1)S(1)}, u32[]{:S(2)}, u32[]{:S(2)}) collective-permute-start(bf16[127,1024]{1,0:T(8,128)(2,1)S(1)} %slice_bitcast_fusion), channel_id=1, source_target_pairs={{0,8},{8,16},{16,24},{24,32},{32,40},{40,48},{48,56},{56,64},{64,7... | collective-permute-start | bytes 780296 | tf_op jit(solution)/shard_map/ppermute | solution.py:18
  9.1 116.6 %collective-permute-start = (bf16[1,256,1024]{1,2,0:T(8,128)(2,1)}, bf16[1,256,1024]{1,2,0:T(8,128)(2,1)}, u32[]{:S(2)}, u32[]{:S(2)}) collective-permute-start(bf16[1,256,1024]{1,2,0:T(8,128)(2,1)} %copy.26), channel_id=1, source_target_pairs={{128,0},{256,128},{384,256},{0,384},{129,1},{257,129},{385,257},{1... | collective-permute-start | bytes 1572872 | tf_op jit(solution)/shard_map/ppermute | solution.py:12
  23.8 15.9 %copy-start.1 = (bf16[1,256,1024]{2,1,0:T(8,128)(2,1)S(1)}, bf16[1,256,1024]{2,1,0:T(8,128)(2,1)}, u32[]{:S(2)}) copy-start(bf16[1,256,1024]{2,1,0:T(8,128)(2,1)} %param.12) | copy-start | bytes 1572868
  132.1 127.2 %collective-permute-start.1 = (f32[127,1024]{0,1:T(8,128)}, f32[127,1024]{0,1:T(8,128)}, u32[]{:S(2)}, u32[]{:S(2)}) collective-permute-start(f32[127,1024]{0,1:T(8,128)} %bitcast.11), channel_id=1, source_target_pairs={{8,0},{16,8},{24,16},{32,24},{40,32},{48,40},{56,48},{64,56},{72,6... | collective-permute-start | bytes 1560584 | tf_op jit(solution)/shard_map/ppermute | solution.py:18
  177.5 30.9 %copy-start = (bf16[1,256,1024]{1,2,0:T(8,128)(2,1)S(1)}, bf16[1,256,1024]{1,2,0:T(8,128)(2,1)}, u32[]{:S(2)}) copy-start(bf16[1,256,1024]{1,2,0:T(8,128)(2,1)} %get-tuple-element.359) | copy-start | bytes 1572868
where the time goes:
time: 265 us; the launch traced here: 262 us
  local copies, waits for them, and re-layouts  162 us (61%)
  blocking collectives  49.9 us (19%)
  matrix products  26.9 us (10%)
  starting transfers between devices  12 us (5%)
  other arithmetic  6.92 us (3%)
  loops' own time  3.32 us (1%)
    psum x1, blocking collectives, body(): filter_grad = lax.psum(partial_filter, 'ctx')  49.9 us
    reshape x3, local copies, waits for them, and re-layouts, skew_table(): return tiled.reshape(groups, nout, win)  47.8 us
    dynamic_update_slice x4, local copies, waits for them, and re-layouts, forward_conv(): out = lax.map(forward_one, jnp.arange(rows // blk, dtype=jnp.int32))  41.6 us
    reshape x2, local copies, waits for them, and re-layouts, lag_sums(): flat = product.reshape(groups, blk * win)  18.5 us
    unnamed x11, local copies, waits for them, and re-layouts  11.5 us
    another operation x4, local copies, waits for them, and re-layouts, skew_table(): tiled = jnp.tile(padded, (1, nout))[:, :nout * win]  11.4 us
    dot_general x3, matrix products, upward(): jnp.einsum('gij,jgc->igc', weights, grad_window, preferred_element_type=j...  11 us
    dot_general x2, matrix products, step(): jnp.einsum('igc,jgc->gij', part, window, preferred_element_type=jnp.float32)  9.05 us
  transfers between devices with their start and end apart: 3, of which 0 were waited for; matrix products, arithmetic and copies ran while one was open for 71% of the time, Pallas kernels for 0%

commit v1 on v0

v1 whole, which is shorter than its diff:
```python
import functools

import jax
import jax.numpy as jnp
from jax import lax
from jax.experimental import pallas as pl
from jax.experimental.pallas import tpu as pltpu
from jax.sharding import PartitionSpec as P

MESH = pl.DeviceIdType.MESH
TILE = 128
F32 = jnp.float32
BF16 = jnp.bfloat16
LAG = 2


def iota(shape, axis):
    return lax.broadcasted_iota(jnp.int32, shape, axis)


def owner_of(position, starts):
    owner = jnp.zeros_like(position)
    for start in starts[1:]:
        owner = jnp.where(position >= start, start, owner)
    return owner


def dot(left, right, contract):
    return lax.dot_general(left, right, ((contract[0], contract[1]), ((), ())), preferred_element_type=F32)


def kernel(
    n_pipe, n_ctx, chans,
    values, gates, incoming, filters, lengths,
    value_grad, gate_grad, filter_grad,
    v_all, g_all, og, cg_all, conv, gg, vg, filt, lens,
    mask_c, mask_t, mask_q, ahead, back, lhs_c, lhs_t, lhs_p, part, gathered, total,
    load_sem, og_send, og_recv, vh_send, vh_recv, ch_send, ch_recv,
    rs_send, rs_recv, ag_send, ag_recv, out_sem, last_sem,
):
    pipe, me = lax.axis_index("pipe"), lax.axis_index("ctx")
    rows, width = g_all.shape
    blocks = rows // TILE
    tiles = width // TILE
    per = TILE // chans
    groups = filt.shape[0]
    piece = groups // n_ctx
    pipe_prev = lax.rem(pipe + n_pipe - 1, n_pipe)
    pipe_next = lax.rem(pipe + 1, n_pipe)
    prev, nxt = lax.rem(me + n_ctx - 1, n_ctx), lax.rem(me + 1, n_ctx)

    loads = [
        pltpu.make_async_copy(values.at[0], v_all.at[pl.ds(TILE, rows)], load_sem.at[0]),
        pltpu.make_async_copy(gates.at[0], g_all, load_sem.at[1]),
        pltpu.make_async_copy(filters.at[0], filt, load_sem.at[2]),
        pltpu.make_async_copy(lengths, lens, load_sem.at[3]),
    ]
    for load in loads:
        load.start()

    barrier = pltpu.get_barrier_semaphore()
    pl.semaphore_signal(barrier, inc=1, device_id={"pipe": pipe_prev}, device_id_type=MESH)
    pl.semaphore_signal(barrier, inc=1, device_id={"pipe": pipe_next}, device_id_type=MESH)

    def greet(d, carry):
        other = lax.rem(me + d, n_ctx)
        pl.semaphore_signal(barrier, inc=1, device_id={"ctx": other}, device_id_type=MESH)
        return carry

    lax.fori_loop(1, n_ctx, greet, 0)
    pl.semaphore_wait(barrier, n_ctx + 1)

    def columns(ct):
        return pl.ds(pl.multiple_of(ct * TILE, TILE), TILE)

    def og_copy(ct):
        return pltpu.make_async_remote_copy(
            src_ref=incoming.at[0, :, columns(ct)], dst_ref=og.at[:, columns(ct)],
            send_sem=og_send.at[ct], recv_sem=og_recv.at[ct],
            device_id={"pipe": pipe_prev}, device_id_type=MESH,
        )

    def ch_copy(ct):
        return pltpu.make_async_remote_copy(
            src_ref=cg_all.at[pl.ds(0, TILE), columns(ct)],
            dst_ref=cg_all.at[pl.ds(rows, TILE), columns(ct)],
            send_sem=ch_send.at[ct], recv_sem=ch_recv.at[ct],
            device_id={"ctx": prev}, device_id_type=MESH,
        )

    def gg_out(ct):
        return pltpu.make_async_copy(gg.at[:, columns(ct)], gate_grad.at[0, :, columns(ct)], out_sem.at[0, ct])

    def vg_out(ct):
        return pltpu.make_async_copy(vg.at[:, columns(ct)], value_grad.at[0, :, columns(ct)], out_sem.at[1, ct])

    halo = pltpu.make_async_remote_copy(
        src_ref=values.at[0, pl.ds(rows - TILE, TILE)], dst_ref=v_all.at[pl.ds(0, TILE)],
        send_sem=vh_send, recv_sem=vh_recv, device_id={"ctx": nxt}, device_id_type=MESH,
    )
    halo.start()

    def og_start(ct, carry):
        og_copy(ct).start()
        return carry

    lax.fori_loop(0, tiles, og_start, 0)

    loads[3].wait()
    starts, at = [], 0
    for d in range(lens.shape[0]):
        starts.append(at)
        at = at + lens[d]
    first = me * rows
    low = iota((TILE, TILE), 0)
    lane = iota((TILE, TILE), 1)
    for b in range(blocks):
        begin = first + b * TILE
        owner = owner_of(begin + low, starts)
        before = (lane > low) & (begin - TILE + lane >= owner)
        same = (lane <= low) & (begin + lane >= owner)
        mask_q[b, :, :TILE] = jnp.where(before, 1.0, 0.0)
        mask_q[b, :, TILE:] = jnp.where(same, 1.0, 0.0)
        mask_c[b, :, :TILE] = jnp.where(before, 1.0, 0.0).astype(BF16)
        mask_c[b, :, TILE:] = jnp.where(same, 1.0, 0.0).astype(BF16)
        source = begin + low
        for half in range(2):
            target = begin + half * TILE + lane
            side = (lane >= low) if half == 0 else (lane < low)
            keep = side & (source >= owner_of(target, starts)) & (target < n_ctx * rows)
            mask_t[b, :, half * TILE:(half + 1) * TILE] = jnp.where(keep, 1.0, 0.0).astype(BF16)

    loads[2].wait()
    flip = jnp.where(lax.rem(low + lane, TILE) == 0, 1.0, 0.0)
    taps = filt[...]
    ahead[...] = taps.astype(F32).reshape(ahead.shape)
    back[...] = dot(taps, flip.astype(BF16), ((1,), (0,))).reshape(back.shape)

    def circulant(row):
        spread = jnp.broadcast_to(row, (TILE, TILE))
        return pltpu.roll(spread, 0, 1, stride=1, stride_axis=0).astype(BF16)

    lane_group = lane // chans

    def pick(product):
        out = product[0:TILE]
        for g in range(1, per):
            out = jnp.where(lane_group >= g, product[g * TILE:(g + 1) * TILE], out)
        return out

    loads[0].wait()
    halo.wait_recv()

    def conv_step(ct, carry):
        rev = back[ct]
        for g in range(per):
            tile = circulant(rev[g:g + 1])
            for b in range(blocks):
                lhs_c[b, g * TILE:(g + 1) * TILE, :TILE] = tile * mask_c[b, :, :TILE]
                lhs_c[b, g * TILE:(g + 1) * TILE, TILE:] = tile * mask_c[b, :, TILE:]
        for b in range(blocks):
            window = v_all[b * TILE:(b + 2) * TILE, columns(ct)]
            conv[b * TILE:(b + 1) * TILE, columns(ct)] = pick(dot(lhs_c[b], window, ((1,), (0,))))
        fwd = ahead[ct]
        for g in range(per):
            tile = circulant(fwd[g:g + 1])
            for b in range(blocks):
                lhs_t[ct, b, g * TILE:(g + 1) * TILE, :TILE] = tile * mask_t[b, :, :TILE]
                lhs_t[ct, b, g * TILE:(g + 1) * TILE, TILE:] = tile * mask_t[b, :, TILE:]
        return carry

    lax.fori_loop(0, tiles, conv_step, 0)
    loads[1].wait()

    def value_step(ct):
        ch_copy(ct).wait_recv()
        for b in range(blocks):
            window = cg_all[b * TILE:(b + 2) * TILE, columns(ct)]
            vg[b * TILE:(b + 1) * TILE, columns(ct)] = pick(dot(lhs_t[ct, b], window, ((1,), (0,)))).astype(BF16)
        vg_out(ct).start()

    sub = iota((per * 8, TILE), 0) % 8

    def main_step(ct, carry):
        og_copy(ct).wait_recv()
        grad = og[:, columns(ct)].astype(F32)
        cg_all[0:rows, columns(ct)] = (grad * g_all[:, columns(ct)].astype(F32)).astype(BF16)
        ch_copy(ct).start()
        gg[:, columns(ct)] = (grad * conv[:, columns(ct)]).astype(BF16)
        gg_out(ct).start()
        for b in range(blocks):
            own = cg_all[b * TILE:(b + 1) * TILE, columns(ct)]
            for g in range(per):
                keep = (lane_group == g).astype(F32).astype(BF16)
                lhs_p[b, g * TILE:(g + 1) * TILE] = own * keep
        products = []
        for b in range(blocks):
            window = v_all[b * TILE:(b + 2) * TILE, columns(ct)]
            products.append(dot(lhs_p[b], window, ((1,), (1,))))
        skewed = []
        for g in range(per):
            acc = jnp.zeros((8, TILE), F32)
            for a in range(TILE // 8):
                at = slice(a * 8, a * 8 + 8)
                row = slice(g * TILE + a * 8, g * TILE + a * 8 + 8)
                both = jnp.zeros((8, TILE), F32)
                for b in range(blocks):
                    both = both + products[b][row, :TILE] * mask_q[b, at, :TILE]
                    both = both + products[b][row, TILE:] * mask_q[b, at, TILE:]
                acc = acc + pltpu.roll(both, (TILE - 8 * a) % TILE, 1)
            skewed.append(acc)
        table = jnp.concatenate(skewed, axis=0)
        for bit in (1, 2, 4):
            table = jnp.where(sub & bit != 0, pltpu.roll(table, TILE - bit, 1), table)
        sums = jnp.sum(table.reshape(per, 8, TILE), axis=1)
        if piece >= per:
            part[ct // (piece // per), pl.ds(lax.rem(ct, piece // per) * per, per)] = sums
        else:
            for q in range(per // piece):
                part[ct * (per // piece) + q] = sums[q * piece:(q + 1) * piece]

        @pl.when(ct >= LAG)
        def _():
            value_step(ct - LAG)

        return carry

    lax.fori_loop(0, tiles, main_step, 0)

    def rs_copy(to, slot):
        return pltpu.make_async_remote_copy(
            src_ref=part.at[to], dst_ref=gathered.at[slot],
            send_sem=rs_send.at[to], recv_sem=rs_recv.at[slot],
            device_id={"ctx": to}, device_id_type=MESH,
        )

    def ag_copy(to, slot):
        return pltpu.make_async_remote_copy(
            src_ref=total.at[me], dst_ref=total.at[slot],
            send_sem=ag_send.at[to], recv_sem=ag_recv.at[slot],
            device_id={"ctx": to}, device_id_type=MESH,
        )

    def others(act):
        def step(d, carry):
            act(lax.rem(me + d, n_ctx))
            return carry

        lax.fori_loop(1, n_ctx, step, 0)

    others(lambda to: rs_copy(to, me).start())
    gathered[me] = part[me]
    for ct in range(tiles - LAG, tiles - 1):
        value_step(ct)
    others(lambda source: rs_copy(source, source).wait_recv())
    summed = jnp.sum(gathered[...], axis=0)
    total[me] = lax.dot_general(
        summed, flip, (((1,), (0,)), ((), ())), precision=lax.Precision.HIGHEST, preferred_element_type=F32
    )
    others(lambda to: ag_copy(to, me).start())
    value_step(tiles - 1)
    others(lambda source: ag_copy(source, source).wait_recv())
    last = pltpu.make_async_copy(total, filter_grad, last_sem)
    last.start()

    halo.wait_send()

    def finish(ct, carry):
        og_copy(ct).wait_send()
        ch_copy(ct).wait_send()
        gg_out(ct).wait()
        vg_out(ct).wait()
        return carry

    lax.fori_loop(0, tiles, finish, 0)
    others(lambda to: rs_copy(to, me).wait_send())
    others(lambda to: ag_copy(to, me).wait_send())
    last.wait()


def solution(mesh):
    n_pipe, n_ctx = mesh.shape["pipe"], mesh.shape["ctx"]

    def body(values, gates, incoming, filters, lengths):
        _, rows, width = values.shape
        _, groups, taps = filters.shape
        tiles, blocks = width // TILE, rows // TILE
        chans = width // groups
        per = TILE // chans
        piece = groups // n_ctx
        dma = pltpu.SemaphoreType.DMA
        any_spec = pl.BlockSpec(memory_space=pl.ANY)
        value_grad, gate_grad, filter_grad = pl.pallas_call(
            functools.partial(kernel, n_pipe, n_ctx, chans),
            out_shape=(
                jax.ShapeDtypeStruct(values.shape, BF16),
                jax.ShapeDtypeStruct(values.shape, BF16),
                jax.ShapeDtypeStruct((n_ctx, piece, taps), F32),
            ),
            in_specs=[any_spec] * 5,
            out_specs=(any_spec,) * 3,
            scratch_shapes=[
                pltpu.VMEM((rows + TILE, width), BF16),
                pltpu.VMEM((rows, width), BF16),
                pltpu.VMEM((rows, width), BF16),
                pltpu.VMEM((rows + TILE, width), BF16),
                pltpu.VMEM((rows, width), F32),
                pltpu.VMEM((rows, width), BF16),
                pltpu.VMEM((rows, width), BF16),
                pltpu.VMEM((groups, taps), BF16),
                pltpu.SMEM(lengths.shape, jnp.int32),
                pltpu.VMEM((blocks, TILE, 2 * TILE), BF16),
                pltpu.VMEM((blocks, TILE, 2 * TILE), BF16),
                pltpu.VMEM((blocks, TILE, 2 * TILE), F32),
                pltpu.VMEM((tiles, per, taps), F32),
                pltpu.VMEM((tiles, per, taps), F32),
                pltpu.VMEM((blocks, per * TILE, 2 * TILE), BF16),
                pltpu.VMEM((tiles, blocks, per * TILE, 2 * TILE), BF16),
                pltpu.VMEM((blocks, per * TILE, TILE), BF16),
                pltpu.VMEM((n_ctx, piece, taps), F32),
                pltpu.VMEM((n_ctx, piece, taps), F32),
                pltpu.VMEM((n_ctx, piece, taps), F32),
                dma((4,)),
                dma((tiles,)), dma((tiles,)),
                dma, dma,
                dma((tiles,)), dma((tiles,)),
                dma((n_ctx,)), dma((n_ctx,)),
                dma((n_ctx,)), dma((n_ctx,)),
                dma((2, tiles)), dma,
            ],
            compiler_params=pltpu.CompilerParams(
                collective_id=0, has_side_effects=True, vmem_limit_bytes=48 * 1024 * 1024
            ),
            cost_estimate=pl.CostEstimate(
                flops=2 * 3 * groups * blocks * TILE * 2 * TILE * TILE,
                bytes_accessed=5 * rows * width * 2, transcendentals=0,
            ),
        )(values, gates, incoming, filters, lengths)
        return value_grad, gate_grad, filter_grad.reshape(filters.shape)

    shards = P("pipe", "ctx", "tp")
    taps = P("pipe", "tp", None)
    return jax.shard_map(
        body, mesh=mesh, in_specs=(shards, shards, shards, taps, P()), out_specs=(shards, shards, taps), check_vma=False
    )
```

time: 265 us -> 49.4 us (0.19); the launches traced: 262 us -> 49.1 us
  local copies, waits for them, and re-layouts: 162 us -> 6.69 us
  blocking collectives: 49.9 us -> 0 us
  Pallas kernels: 0 us -> 41.7 us
  matrix products: 26.9 us -> 0 us
  starting transfers between devices: 12 us -> 0 us
  other arithmetic: 6.92 us -> 0 us
  loops' own time: 3.32 us -> 0 us
    reshape x6 -> x0, local copies, waits for them, and re-layouts: 67.1 us -> none  [the longest x3 47.8 us: skew_table(): return tiled.reshape(groups, nout, win)]
    psum x1 -> x0, blocking collectives: 49.9 us -> none  [body(): filter_grad = lax.psum(partial_filter, 'ctx')]
    pallas_call x0 -> x1, Pallas kernels: none -> 41.7 us  [body(): pl.pallas_call(functools.partial(kernel, n_pipe, n_ctx, chans), out_shape...]
    dynamic_update_slice x4 -> x0, local copies, waits for them, and re-layouts: 41.6 us -> none  [forward_conv(): out = lax.map(forward_one, jnp.arange(rows // blk, dtype=jnp.int32))]
    dot_general x7 -> x0, matrix products: 26.9 us -> none  [the longest x3 11 us: upward(): jnp.einsum('gij,jgc->igc', weights, grad_window, preferred_element_type=j...]
    another operation x7 -> x0, local copies, waits for them, and re-layouts: 13.1 us -> none  [the longest x4 11.4 us: skew_table(): tiled = jnp.tile(padded, (1, nout))[:, :nout * win]]
    ppermute x3 -> x0, starting transfers between devices: 12 us -> none  [the longest x2 7.62 us: shifted_2(): return lax.ppermute(value, axis, pairs)]
    slice x5 -> x0, local copies, waits for them, and re-layouts: 9.91 us -> none  [the longest x3 8.88 us: skew_table(): tiled = jnp.tile(padded, (1, nout))[:, :nout * win]]
  transfers between devices with their start and end apart: 3 -> 0, of which waited for: 0 -> 0; matrix products, arithmetic and copies ran while one was open for 71% -> 0% of each run, Pallas kernels for 0% -> 0%
where the time goes in v1:
time: 49.4 us; the launch traced here: 49.1 us
  Pallas kernels  41.7 us (84%)
  local copies, waits for them, and re-layouts  6.69 us (14%)
  between operations  0.65 us (1%)
    pallas_call x1, Pallas kernels, body(): pl.pallas_call(functools.partial(kernel, n_pipe, n_ctx, chans), out_shape...  41.7 us
    unnamed x13, local copies, waits for them, and re-layouts  6.69 us

profile of v1, /device:TPU:1, one launch (start us, length us, event | category | flops | bytes accessed | tf_op | source)
XLA Modules:
  0.0 49.1 jit_solution(9987714337043995743)
XLA Ops:
  0.6 0.0 copy-start
  0.6 1.0 %copy-done = bf16[1,256,1024]{2,1,0:T(8,128)(2,1)S(1)} copy-done((bf16[1,256,1024]{2,1,0:T(8,128)(2,1)S(1)}, bf16[1,256,1024]{2,1,0:T(8,128)(2,1)}, u32[]{:S(2)}) %copy-start) | copy-done | bytes 524312
  1.7 0.0 copy-start.1
  1.7 1.0 %copy-done.1 = bf16[1,256,1024]{2,1,0:T(8,128)(2,1)S(1)} copy-done((bf16[1,256,1024]{2,1,0:T(8,128)(2,1)S(1)}, bf16[1,256,1024]{2,1,0:T(8,128)(2,1)}, u32[]{:S(2)}) %copy-start.1) | copy-done | bytes 524312
  2.7 0.0 copy-start.2
  2.7 1.0 %copy-done.2 = bf16[1,256,1024]{2,1,0:T(8,128)(2,1)S(1)} copy-done((bf16[1,256,1024]{2,1,0:T(8,128)(2,1)S(1)}, bf16[1,256,1024]{2,1,0:T(8,128)(2,1)}, u32[]{:S(2)}) %copy-start.2) | copy-done | bytes 524312
  3.8 0.0 copy-start.3
  3.8 0.7 %copy-done.3 = bf16[1,64,128]{2,1,0:T(8,128)(2,1)S(1)} copy-done((bf16[1,64,128]{2,1,0:T(8,128)(2,1)S(1)}, bf16[1,64,128]{2,1,0:T(8,128)(2,1)}, u32[]{:S(2)}) %copy-start.3) | copy-done | bytes 16408
  4.5 0.0 copy-start.4
  4.5 0.7 %copy-done.4 = s32[16]{0:T(128)S(1)} copy-done((s32[16]{0:T(128)S(1)}, s32[16]{0:T(128)}, u32[]{:S(2)}) %copy-start.4) | copy-done | bytes 88
  5.1 41.7 %shard_map.76 = (bf16[1,256,1024]{2,1,0:T(8,128)(2,1)S(1)}, bf16[1,256,1024]{2,1,0:T(8,128)(2,1)S(1)}, f32[16,4,128]{2,1,0:T(4,128)S(1)}) custom-call(bf16[1,256,1024]{2,1,0:T(8,128)(2,1)S(1)} %copy-done, bf16[1,256,1024]{2,1,0:T(8,128)(2,1)S(1)} %copy-done.1, bf16[1,256,1024]{2,1,0:T(8,128)(2,1)S(1)} %copy-done.2, bf16[1,64,128]{2,1,0:T(8,128)(2,1)S(1)} %copy-done.3, ...), custom_call_target="tpu_custom_call" | custom-call | flops 3221225472 | bytes 2621440 | tf_op jit(solution)/shard_map/pallas_call | solution.py:293
  46.9 0.8 %copy.11 = bf16[1,256,1024]{2,1,0:T(8,128)(2,1)} copy(bf16[1,256,1024]{2,1,0:T(8,128)(2,1)S(1)} %get-tuple-element.12) | data formatting | bytes 1048576
  47.7 0.8 %copy.12 = bf16[1,256,1024]{2,1,0:T(8,128)(2,1)} copy(bf16[1,256,1024]{2,1,0:T(8,128)(2,1)S(1)} %get-tuple-element.13) | data formatting | bytes 1048576
  48.5 0.6 %copy.13 = f32[1,64,128]{2,1,0:T(8,128)} copy(f32[1,64,128]{2,1,0:T(8,128)S(1)} %bitcast.1) | data formatting | bytes 65536
Async XLA Ops:
  0.6 1.0 %copy-start = (bf16[1,256,1024]{2,1,0:T(8,128)(2,1)S(1)}, bf16[1,256,1024]{2,1,0:T(8,128)(2,1)}, u32[]{:S(2)}) copy-start(bf16[1,256,1024]{2,1,0:T(8,128)(2,1)} %values.1) | copy-start | bytes 1572868
  1.7 1.0 %copy-start.1 = (bf16[1,256,1024]{2,1,0:T(8,128)(2,1)S(1)}, bf16[1,256,1024]{2,1,0:T(8,128)(2,1)}, u32[]{:S(2)}) copy-start(bf16[1,256,1024]{2,1,0:T(8,128)(2,1)} %gates.1) | copy-start | bytes 1572868
  2.7 1.0 %copy-start.2 = (bf16[1,256,1024]{2,1,0:T(8,128)(2,1)S(1)}, bf16[1,256,1024]{2,1,0:T(8,128)(2,1)}, u32[]{:S(2)}) copy-start(bf16[1,256,1024]{2,1,0:T(8,128)(2,1)} %incoming.1) | copy-start | bytes 1572868
  3.8 0.7 %copy-start.3 = (bf16[1,64,128]{2,1,0:T(8,128)(2,1)S(1)}, bf16[1,64,128]{2,1,0:T(8,128)(2,1)}, u32[]{:S(2)}) copy-start(bf16[1,64,128]{2,1,0:T(8,128)(2,1)} %filters.1) | copy-start | bytes 49156
  4.5 0.7 %copy-start.4 = (s32[16]{0:T(128)S(1)}, s32[16]{0:T(128)}, u32[]{:S(2)}) copy-start(s32[16]{0:T(128)} %lengths.1) | copy-start | bytes 196

commit v2 on v1

--- a/solution.py
+++ b/solution.py
@@ -11,7 +11,6 @@
 TILE = 128
 F32 = jnp.float32
 BF16 = jnp.bfloat16
-LAG = 2
 
 
 def iota(shape, axis):
@@ -34,9 +33,9 @@
     values, gates, incoming, filters, lengths,
     value_grad, gate_grad, filter_grad,
     v_all, g_all, og, cg_all, conv, gg, vg, filt, lens,
-    mask_c, mask_t, mask_q, ahead, back, lhs_c, lhs_t, lhs_p, part, gathered, total,
+    mask_c, mask_t, mask_q, ahead, back, lhs_c, lhs_t, lhs_p, slots, mine, theirs, total,
     load_sem, og_send, og_recv, vh_send, vh_recv, ch_send, ch_recv,
-    rs_send, rs_recv, ag_send, ag_recv, out_sem, last_sem,
+    z_send, z_recv, pair_send, pair_recv, out_sem, last_sem, near_sem,
 ):
     pipe, me = lax.axis_index("pipe"), lax.axis_index("ctx")
     rows, width = g_all.shape
@@ -44,7 +43,9 @@
     tiles = width // TILE
     per = TILE // chans
     groups = filt.shape[0]
-    piece = groups // n_ctx
+    n_z = n_ctx // 2
+    z = me // 2
+    partner = me + 1 - 2 * (me % 2)
     pipe_prev = lax.rem(pipe + n_pipe - 1, n_pipe)
     pipe_next = lax.rem(pipe + 1, n_pipe)
     prev, nxt = lax.rem(me + n_ctx - 1, n_ctx), lax.rem(me + 1, n_ctx)
@@ -62,13 +63,20 @@
     pl.semaphore_signal(barrier, inc=1, device_id={"pipe": pipe_prev}, device_id_type=MESH)
     pl.semaphore_signal(barrier, inc=1, device_id={"pipe": pipe_next}, device_id_type=MESH)
 
-    def greet(d, carry):
-        other = lax.rem(me + d, n_ctx)
-        pl.semaphore_signal(barrier, inc=1, device_id={"ctx": other}, device_id_type=MESH)
-        return carry
-
-    lax.fori_loop(1, n_ctx, greet, 0)
-    pl.semaphore_wait(barrier, n_ctx + 1)
+    pl.semaphore_signal(barrier, inc=1, device_id={"ctx": prev}, device_id_type=MESH)
+    pl.semaphore_signal(barrier, inc=1, device_id={"ctx": nxt}, device_id_type=MESH)
+    pl.semaphore_wait(barrier, 4)
+
+    rounds = (n_ctx // 2).bit_length() - 1
+
+    def tell(r):
+        for other in (me + n_ctx - (1 << r), me + (1 << r)):
+            pl.semaphore_signal(near_sem.at[r], inc=1, device_id={"ctx": lax.rem(other, n_ctx)}, device_id_type=MESH)
+
+    def hear(r):
+        pl.semaphore_wait(near_sem.at[r], 2)
+        if r + 1 < rounds:
+            tell(r + 1)
 
     def columns(ct):
         return pl.ds(pl.multiple_of(ct * TILE, TILE), TILE)
@@ -100,11 +108,9 @@
     )
     halo.start()
 
-    def og_start(ct, carry):
-        og_copy(ct).start()
-        return carry
-
-    lax.fori_loop(0, tiles, og_start, 0)
+    og_copy(0).start()
+    og_copy(1).start()
+    tell(0)
 
     loads[3].wait()
     starts, at = [], 0
@@ -149,27 +155,42 @@
         return out
 
     loads[0].wait()
-    halo.wait_recv()
+
+    def convolve(ct, b):
+        window = v_all[b * TILE:(b + 2) * TILE, columns(ct)]
+        conv[b * TILE:(b + 1) * TILE, columns(ct)] = pick(dot(lhs_c[ct, b], window, ((1,), (0,))))
 
     def conv_step(ct, carry):
-        rev = back[ct]
+        @pl.when((ct == 2) | (ct == 5))
+        def _():
+            og_copy(ct // 5 + 2).start()
+
+        for r in range(rounds - 1):
+            pl.when(ct == 3 * r + 2)(functools.partial(hear, r))
+
+        rev, fwd = back[ct], ahead[ct]
         for g in range(per):
+            at = slice(g * TILE, (g + 1) * TILE)
             tile = circulant(rev[g:g + 1])
             for b in range(blocks):
-                lhs_c[b, g * TILE:(g + 1) * TILE, :TILE] = tile * mask_c[b, :, :TILE]
-                lhs_c[b, g * TILE:(g + 1) * TILE, TILE:] = tile * mask_c[b, :, TILE:]
-        for b in range(blocks):
-            window = v_all[b * TILE:(b + 2) * TILE, columns(ct)]
-            conv[b * TILE:(b + 1) * TILE, columns(ct)] = pick(dot(lhs_c[b], window, ((1,), (0,))))
-        fwd = ahead[ct]
-        for g in range(per):
+                lhs_c[ct, b, at, :TILE] = tile * mask_c[b, :, :TILE]
+                lhs_c[ct, b, at, TILE:] = tile * mask_c[b, :, TILE:]
             tile = circulant(fwd[g:g + 1])
             for b in range(blocks):
-                lhs_t[ct, b, g * TILE:(g + 1) * TILE, :TILE] = tile * mask_t[b, :, :TILE]
-                lhs_t[ct, b, g * TILE:(g + 1) * TILE, TILE:] = tile * mask_t[b, :, TILE:]
+                lhs_t[ct, b, at, :TILE] = tile * mask_t[b, :, :TILE]
+                lhs_t[ct, b, at, TILE:] = tile * mask_t[b, :, TILE:]
+        for b in range(1, blocks):
+            convolve(ct, b)
+        return carry
+
+    def first_step(ct, carry):
+        convolve(ct, 0)
         return carry
 
     lax.fori_loop(0, tiles, conv_step, 0)
+    halo.wait_recv()
+    lax.fori_loop(0, tiles, first_step, 0)
+    hear(rounds - 1)
     loads[1].wait()
 
     def value_step(ct):
@@ -179,9 +200,41 @@
             vg[b * TILE:(b + 1) * TILE, columns(ct)] = pick(dot(lhs_t[ct, b], window, ((1,), (0,)))).astype(BF16)
         vg_out(ct).start()
 
+    def z_copy(ct, k):
+        return pltpu.make_async_remote_copy(
+            src_ref=slots.at[ct, z], dst_ref=slots.at[ct, z],
+            send_sem=z_send.at[ct, k], recv_sem=z_recv.at[ct, k],
+            device_id={"ctx": lax.rem(me + 2 * k, n_ctx)}, device_id_type=MESH,
+        )
+
+    def z_wait(ct, k):
+        source = lax.rem(z + n_z - k, n_z)
+        pltpu.make_async_remote_copy(
+            src_ref=slots.at[ct, source], dst_ref=slots.at[ct, source],
+            send_sem=z_send.at[ct, k], recv_sem=z_recv.at[ct, k],
+            device_id={"ctx": lax.rem(me + 2 * k, n_ctx)}, device_id_type=MESH,
+        ).wait_recv()
+
+    def pair_copy(ct):
+        return pltpu.make_async_remote_copy(
+            src_ref=mine.at[ct], dst_ref=theirs.at[ct],
+            send_sem=pair_send.at[ct], recv_sem=pair_recv.at[ct],
+            device_id={"ctx": partner}, device_id_type=MESH,
+        )
+
+    def column_sum(ct):
+        for k in range(1, n_z):
+            z_wait(ct, k)
+        mine[ct] = jnp.sum(slots[ct], axis=0)
+        pair_copy(ct).start()
+
     sub = iota((per * 8, TILE), 0) % 8
 
     def main_step(ct, carry):
+        @pl.when(ct < tiles - 4)
+        def _():
+            og_copy(ct + 4).start()
+
         og_copy(ct).wait_recv()
         grad = og[:, columns(ct)].astype(F32)
         cg_all[0:rows, columns(ct)] = (grad * g_all[:, columns(ct)].astype(F32)).astype(BF16)
@@ -213,54 +266,29 @@
         for bit in (1, 2, 4):
             table = jnp.where(sub & bit != 0, pltpu.roll(table, TILE - bit, 1), table)
         sums = jnp.sum(table.reshape(per, 8, TILE), axis=1)
-        if piece >= per:
-            part[ct // (piece // per), pl.ds(lax.rem(ct, piece // per) * per, per)] = sums
-        else:
-            for q in range(per // piece):
-                part[ct * (per // piece) + q] = sums[q * piece:(q + 1) * piece]
-
-        @pl.when(ct >= LAG)
-        def _():
-            value_step(ct - LAG)
+        slots[ct, z] = sums
+        for k in range(1, n_z):
+            z_copy(ct, k).start()
 
         return carry
 
     lax.fori_loop(0, tiles, main_step, 0)
 
-    def rs_copy(to, slot):
-        return pltpu.make_async_remote_copy(
-            src_ref=part.at[to], dst_ref=gathered.at[slot],
-            send_sem=rs_send.at[to], recv_sem=rs_recv.at[slot],
-            device_id={"ctx": to}, device_id_type=MESH,
-        )
-
-    def ag_copy(to, slot):
-        return pltpu.make_async_remote_copy(
-            src_ref=total.at[me], dst_ref=total.at[slot],
-            send_sem=ag_send.at[to], recv_sem=ag_recv.at[slot],
-            device_id={"ctx": to}, device_id_type=MESH,
-        )
-
-    def others(act):
-        def step(d, carry):
-            act(lax.rem(me + d, n_ctx))
-            return carry
-
-        lax.fori_loop(1, n_ctx, step, 0)
-
-    others(lambda to: rs_copy(to, me).start())
-    gathered[me] = part[me]
-    for ct in range(tiles - LAG, tiles - 1):
+    def tail_step(ct, carry):
         value_step(ct)
-    others(lambda source: rs_copy(source, source).wait_recv())
-    summed = jnp.sum(gathered[...], axis=0)
-    total[me] = lax.dot_general(
-        summed, flip, (((1,), (0,)), ((), ())), precision=lax.Precision.HIGHEST, preferred_element_type=F32
+        column_sum(ct)
+        return carry
+
+    lax.fori_loop(0, tiles - 1, tail_step, 0)
+    value_step(tiles - 1)
+    column_sum(tiles - 1)
+    for ct in range(tiles):
+        pair_copy(ct).wait_recv()
+    both = (mine[...] + theirs[...]).reshape(groups, TILE)
+    total[...] = lax.dot_general(
+        both, flip, (((1,), (0,)), ((), ())), precision=lax.Precision.HIGHEST, preferred_element_type=F32
     )
-    others(lambda to: ag_copy(to, me).start())
-    value_step(tiles - 1)
-    others(lambda source: ag_copy(source, source).wait_recv())
-    last = pltpu.make_async_copy(total, filter_grad, last_sem)
+    last = pltpu.make_async_copy(total, filter_grad.at[0], last_sem)
     last.start()
 
     halo.wait_send()
@@ -270,11 +298,12 @@
         ch_copy(ct).wait_send()
         gg_out(ct).wait()
         vg_out(ct).wait()
+        pair_copy(ct).wait_send()
+        for k in range(1, n_z):
+            z_copy(ct, k).wait_send()
         return carry
 
     lax.fori_loop(0, tiles, finish, 0)
-    others(lambda to: rs_copy(to, me).wait_send())
-    others(lambda to: ag_copy(to, me).wait_send())
     last.wait()
 
 
@@ -287,7 +316,7 @@
         tiles, blocks = width // TILE, rows // TILE
         chans = width // groups
         per = TILE // chans
-        piece = groups // n_ctx
+        n_z = n_ctx // 2
         dma = pltpu.SemaphoreType.DMA
         any_spec = pl.BlockSpec(memory_space=pl.ANY)
         value_grad, gate_grad, filter_grad = pl.pallas_call(
@@ -295,9 +324,9 @@
             out_shape=(
                 jax.ShapeDtypeStruct(values.shape, BF16),
                 jax.ShapeDtypeStruct(values.shape, BF16),
-                jax.ShapeDtypeStruct((n_ctx, piece, taps), F32),
+                jax.ShapeDtypeStruct(filters.shape, F32),
             ),
-            in_specs=[any_spec] * 5,
+            in_specs=[pl.BlockSpec(memory_space=pltpu.HBM)] * 5,
             out_specs=(any_spec,) * 3,
             scratch_shapes=[
                 pltpu.VMEM((rows + TILE, width), BF16),
@@ -314,29 +343,31 @@
                 pltpu.VMEM((blocks, TILE, 2 * TILE), F32),
                 pltpu.VMEM((tiles, per, taps), F32),
                 pltpu.VMEM((tiles, per, taps), F32),
-                pltpu.VMEM((blocks, per * TILE, 2 * TILE), BF16),
+                pltpu.VMEM((tiles, blocks, per * TILE, 2 * TILE), BF16),
                 pltpu.VMEM((tiles, blocks, per * TILE, 2 * TILE), BF16),
                 pltpu.VMEM((blocks, per * TILE, TILE), BF16),
-                pltpu.VMEM((n_ctx, piece, taps), F32),
-                pltpu.VMEM((n_ctx, piece, taps), F32),
-                pltpu.VMEM((n_ctx, piece, taps), F32),
+                pltpu.VMEM((tiles, n_z, per, taps), F32),
+                pltpu.VMEM((tiles, per, taps), F32),
+                pltpu.VMEM((tiles, per, taps), F32),
+                pltpu.VMEM((groups, taps), F32),
                 dma((4,)),
                 dma((tiles,)), dma((tiles,)),
                 dma, dma,
                 dma((tiles,)), dma((tiles,)),
-                dma((n_ctx,)), dma((n_ctx,)),
-                dma((n_ctx,)), dma((n_ctx,)),
+                dma((tiles, n_z)), dma((tiles, n_z)),
+                dma((tiles,)), dma((tiles,)),
                 dma((2, tiles)), dma,
+                pltpu.SemaphoreType.REGULAR((4,)),
             ],
             compiler_params=pltpu.CompilerParams(
-                collective_id=0, has_side_effects=True, vmem_limit_bytes=48 * 1024 * 1024
+                collective_id=0, has_side_effects=True, vmem_limit_bytes=62 * 1024 * 1024
             ),
             cost_estimate=pl.CostEstimate(
                 flops=2 * 3 * groups * blocks * TILE * 2 * TILE * TILE,
                 bytes_accessed=5 * rows * width * 2, transcendentals=0,
             ),
         )(values, gates, incoming, filters, lengths)
-        return value_grad, gate_grad, filter_grad.reshape(filters.shape)
+        return value_grad, gate_grad, filter_grad
 
     shards = P("pipe", "ctx", "tp")
     taps = P("pipe", "tp", None)

time: 49.4 us -> 38.6 us (0.78)
  Pallas kernels: 41.7 us -> 34.5 us
  local copies, waits for them, and re-layouts: 6.69 us -> 3.34 us
    pallas_call x1, Pallas kernels: 41.7 us -> 34.5 us  [body(): pl.pallas_call(functools.partial(kernel, n_pipe, n_ctx, chans), out_shape...]
    unnamed x13 -> x7, local copies, waits for them, and re-layouts: 6.69 us -> 3.34 us
where the time goes in v2:
time: 38.6 us; the launch traced here: 38.5 us
  Pallas kernels  34.5 us (89%)
  local copies, waits for them, and re-layouts  3.34 us (9%)
  between operations  0.65 us (2%)
    pallas_call x1, Pallas kernels, body(): pl.pallas_call(functools.partial(kernel, n_pipe, n_ctx, chans), out_shape...  34.5 us
    unnamed x7, local copies, waits for them, and re-layouts  3.34 us

profile of v2, /device:TPU:1, one launch (start us, length us, event | category | flops | bytes accessed | tf_op | source)
XLA Modules:
  0.0 38.5 jit_solution(1459932889015717201)
XLA Ops:
  0.6 34.5 %shard_map.76 = (bf16[1,256,1024]{2,1,0:T(8,128)(2,1)}, bf16[1,256,1024]{2,1,0:T(8,128)(2,1)}, f32[1,64,128]{2,1,0:T(8,128)}) custom-call(bf16[1,256,1024]{2,1,0:T(8,128)(2,1)} %values.1, bf16[1,256,1024]{2,1,0:T(8,128)(2,1)} %gates.1, bf16[1,256,1024]{2,1,0:T(8,128)(2,1)} %incoming.1, bf16[1,64,128]{2,1,0:T(8,128)(2,1)} %filters.1, s32[16]{0:T(128)} %lengths.1), custom_call_target="tpu_custom_call" | custom-call | flops 3221225472 | bytes 2621440 | tf_op jit(solution)/shard_map/pallas_call | solution.py:322
  35.1 0.0 copy-start
  35.1 1.9 %copy.11 = bf16[1,256,1024]{2,1,0:T(8,128)(2,1)} copy(bf16[1,256,1024]{2,1,0:T(8,128)(2,1)} %get-tuple-element.6) | data formatting | bytes 1048576
  37.0 0.0 copy-done
  37.0 0.0 copy-start.1
  37.0 0.8 %copy.12 = bf16[1,256,1024]{2,1,0:T(8,128)(2,1)} copy(bf16[1,256,1024]{2,1,0:T(8,128)(2,1)S(1)} %copy-done) | data formatting | bytes 1048576
  37.8 0.0 copy-done.1
  37.8 0.6 %copy.13 = f32[1,64,128]{2,1,0:T(8,128)} copy(f32[1,64,128]{2,1,0:T(8,128)S(1)} %copy-done.1) | data formatting | bytes 65536
Async XLA Ops:
  35.1 1.9 %copy-start = (bf16[1,256,1024]{2,1,0:T(8,128)(2,1)S(1)}, bf16[1,256,1024]{2,1,0:T(8,128)(2,1)}, u32[]{:S(2)}) copy-start(bf16[1,256,1024]{2,1,0:T(8,128)(2,1)} %get-tuple-element.7) | copy-start | bytes 1572868
  37.0 0.8 %copy-start.1 = (f32[1,64,128]{2,1,0:T(8,128)S(1)}, f32[1,64,128]{2,1,0:T(8,128)}, u32[]{:S(2)}) copy-start(f32[1,64,128]{2,1,0:T(8,128)} %get-tuple-element.8) | copy-start | bytes 98308

commit v3 on v2

v3 whole, which is shorter than its diff:
```python
import functools

import jax
import jax.numpy as jnp
from jax import lax
from jax.experimental import pallas as pl
from jax.experimental.pallas import tpu as pltpu
from jax.sharding import PartitionSpec as P

MESH = pl.DeviceIdType.MESH
TILE = 128
F32 = jnp.float32
BF16 = jnp.bfloat16


def iota(shape, axis):
    return lax.broadcasted_iota(jnp.int32, shape, axis)


def owner_of(position, starts):
    owner = jnp.zeros_like(position)
    for start in starts[1:]:
        owner = jnp.where(position >= start, start, owner)
    return owner


def dot(left, right, contract):
    return lax.dot_general(left, right, ((contract[0], contract[1]), ((), ())), preferred_element_type=F32)


def kernel(
    n_pipe, n_ctx, chans,
    values, gates, incoming, filters, lengths,
    value_grad, gate_grad, filter_grad,
    v_all, g_all, og, cg_all, conv, filt, lens,
    mask_c, mask_t, mask_q, ahead, back, lhs_a, lhs_b, lhs_c, lhs_t, lhs_p, slots, mine, theirs,
    load_sem, og_send, og_recv, vh_send, vh_recv, ch_send, ch_recv,
    z_send, z_recv, pair_send, pair_recv, near_sem,
):
    pipe, me = lax.axis_index("pipe"), lax.axis_index("ctx")
    rows, width = g_all.shape
    blocks = rows // TILE
    tiles = width // TILE
    per = TILE // chans
    groups = filt.shape[0]
    n_z = n_ctx // 2
    z = me // 2
    partner = me + 1 - 2 * (me % 2)
    pipe_prev = lax.rem(pipe + n_pipe - 1, n_pipe)
    pipe_next = lax.rem(pipe + 1, n_pipe)
    prev, nxt = lax.rem(me + n_ctx - 1, n_ctx), lax.rem(me + 1, n_ctx)

    loads = [
        pltpu.make_async_copy(values.at[0], v_all.at[pl.ds(TILE, rows)], load_sem.at[0]),
        pltpu.make_async_copy(gates.at[0], g_all, load_sem.at[1]),
        pltpu.make_async_copy(filters.at[0], filt, load_sem.at[2]),
        pltpu.make_async_copy(lengths, lens, load_sem.at[3]),
    ]
    for load in loads:
        load.start()

    barrier = pltpu.get_barrier_semaphore()
    pl.semaphore_signal(barrier, inc=1, device_id={"pipe": pipe_prev}, device_id_type=MESH)
    pl.semaphore_signal(barrier, inc=1, device_id={"pipe": pipe_next}, device_id_type=MESH)

    pl.semaphore_signal(barrier, inc=1, device_id={"ctx": prev}, device_id_type=MESH)
    pl.semaphore_signal(barrier, inc=1, device_id={"ctx": nxt}, device_id_type=MESH)
    pl.semaphore_wait(barrier, 4)

    rounds = (n_ctx // 2).bit_length() - 1

    def tell(r):
        for other in (me + n_ctx - (1 << r), me + (1 << r)):
            pl.semaphore_signal(near_sem.at[r], inc=1, device_id={"ctx": lax.rem(other, n_ctx)}, device_id_type=MESH)

    def hear(r):
        pl.semaphore_wait(near_sem.at[r], 2)
        if r + 1 < rounds:
            tell(r + 1)

    def columns(ct):
        return pl.ds(pl.multiple_of(ct * TILE, TILE), TILE)

    def wide(cp):
        return pl.ds(pl.multiple_of(cp * 2 * TILE, 2 * TILE), 2 * TILE)

    def og_copy(ct):
        return pltpu.make_async_remote_copy(
            src_ref=incoming.at[0, :, columns(ct)], dst_ref=og.at[:, columns(ct)],
            send_sem=og_send, recv_sem=og_recv.at[ct],
            device_id={"pipe": pipe_prev}, device_id_type=MESH,
        )

    def ch_copy(cp):
        return pltpu.make_async_remote_copy(
            src_ref=cg_all.at[pl.ds(0, TILE), wide(cp)],
            dst_ref=cg_all.at[pl.ds(rows, TILE), wide(cp)],
            send_sem=ch_send, recv_sem=ch_recv.at[cp],
            device_id={"ctx": prev}, device_id_type=MESH,
        )

    def halo(cp):
        return pltpu.make_async_remote_copy(
            src_ref=values.at[0, pl.ds(rows - TILE, TILE), wide(cp)], dst_ref=v_all.at[pl.ds(0, TILE), wide(cp)],
            send_sem=vh_send, recv_sem=vh_recv.at[cp], device_id={"ctx": nxt}, device_id_type=MESH,
        )

    halo(0).start()
    og_copy(0).start()
    tell(0)
    for cp in range(1, tiles // 2):
        halo(cp).start()
    og_copy(1).start()

    loads[3].wait()
    starts, at = [], 0
    for d in range(lens.shape[0]):
        starts.append(at)
        at = at + lens[d]
    first = me * rows
    low = iota((TILE, TILE), 0)
    lane = iota((TILE, TILE), 1)
    for b in range(blocks):
        begin = first + b * TILE
        owner = owner_of(begin + low, starts)
        before = (lane > low) & (begin - TILE + lane >= owner)
        same = (lane <= low) & (begin + lane >= owner)
        mask_q[b, :, :TILE] = jnp.where(before, 1.0, 0.0)
        mask_q[b, :, TILE:] = jnp.where(same, 1.0, 0.0)
        mask_c[b, :, :TILE] = jnp.where(before, 1.0, 0.0).astype(BF16)
        mask_c[b, :, TILE:] = jnp.where(same, 1.0, 0.0).astype(BF16)
        source = begin + low
        for half in range(2):
            target = begin + half * TILE + lane
            side = (lane >= low) if half == 0 else (lane < low)
            keep = side & (source >= owner_of(target, starts)) & (target < n_ctx * rows)
            mask_t[b, :, half * TILE:(half + 1) * TILE] = jnp.where(keep, 1.0, 0.0).astype(BF16)

    loads[2].wait()
    flip = jnp.where(lax.rem(low + lane, TILE) == 0, 1.0, 0.0)
    taps = filt[...]
    ahead[...] = taps.astype(F32).reshape(ahead.shape)
    back[...] = dot(taps, flip.astype(BF16), ((1,), (0,))).reshape(back.shape)

    def circulant(row):
        spread = jnp.broadcast_to(row, (TILE, TILE))
        return pltpu.roll(spread, 0, 1, stride=1, stride_axis=0).astype(BF16)

    lane_group = lane // chans

    def pick(product):
        out = product[0:TILE]
        for g in range(1, per):
            out = jnp.where(lane_group >= g, product[g * TILE:(g + 1) * TILE], out)
        return out

    loads[0].wait()

    def tables(ct, own):
        rev, fwd = back[ct], ahead[ct]
        for g in range(per):
            at = slice(g * TILE, (g + 1) * TILE)
            tile = circulant(rev[g:g + 1])
            own[at, :TILE] = tile * mask_c[1, :, :TILE]
            own[at, TILE:] = tile * mask_c[1, :, TILE:]
            lhs_c[ct, at, :TILE] = tile * mask_c[0, :, :TILE]
            lhs_c[ct, at, TILE:] = tile * mask_c[0, :, TILE:]
            tile = circulant(fwd[g:g + 1])
            for b in range(blocks):
                lhs_t[ct, b, at, :TILE] = tile * mask_t[b, :, :TILE]
                lhs_t[ct, b, at, TILE:] = tile * mask_t[b, :, TILE:]

    def convolve(ct, b, lhs):
        window = v_all[b * TILE:(b + 2) * TILE, columns(ct)]
        conv[b * TILE:(b + 1) * TILE, columns(ct)] = pick(dot(lhs[...], window, ((1,), (0,))))

    tables(0, lhs_a)

    def conv_step(i, carry):
        @pl.when(i == 1)
        def _():
            og_copy(2).start()
            hear(0)

        tables(2 * i + 1, lhs_b)
        convolve(2 * i, 1, lhs_a)
        tables(2 * i + 2, lhs_a)
        convolve(2 * i + 1, 1, lhs_b)
        return carry

    def first_step(cp, carry):
        halo(cp).wait_recv()
        for j in range(2):
            convolve(2 * cp + j, 0, lhs_c.at[2 * cp + j])
        return carry

    lax.fori_loop(0, tiles // 2 - 1, conv_step, 0)
    og_copy(3).start()
    tables(tiles - 1, lhs_b)
    convolve(tiles - 2, 1, lhs_a)
    convolve(tiles - 1, 1, lhs_b)
    og_copy(4).start()
    hear(1)
    lax.fori_loop(0, tiles // 2, first_step, 0)
    og_copy(5).start()
    loads[1].wait()

    def value_step(cp):
        ch_copy(cp).wait_recv()
        for j in range(2):
            ct = 2 * cp + j
            for b in range(blocks):
                window = cg_all[b * TILE:(b + 2) * TILE, columns(ct)]
                product = dot(lhs_t[ct, b], window, ((1,), (0,)))
                value_grad[0, b * TILE:(b + 1) * TILE, columns(ct)] = pick(product).astype(BF16)

    def z_copy(cp, k):
        return pltpu.make_async_remote_copy(
            src_ref=slots.at[cp, z], dst_ref=slots.at[cp, z],
            send_sem=z_send, recv_sem=z_recv.at[cp],
            device_id={"ctx": lax.rem(me + 2 * k, n_ctx)}, device_id_type=MESH,
        )

    def z_all(cp):
        part = slots.at[cp, pl.ds(0, n_z - 1)]
        return pltpu.make_async_remote_copy(
            src_ref=part, dst_ref=part, send_sem=z_send, recv_sem=z_recv.at[cp],
            device_id={"ctx": nxt}, device_id_type=MESH,
        )

    def pair_copy(cp):
        return pltpu.make_async_remote_copy(
            src_ref=mine.at[cp], dst_ref=theirs.at[cp],
            send_sem=pair_send, recv_sem=pair_recv.at[cp],
            device_id={"ctx": partner}, device_id_type=MESH,
        )

    def column_sum(cp):
        z_all(cp).wait_recv()
        mine[cp] = jnp.sum(slots[cp], axis=0)
        pair_copy(cp).start()

    sub = iota((per * 8, TILE), 0) % 8
    keeps = [(lane_group == g).astype(F32).astype(BF16) for g in range(per)]

    def main_step(cp, carry):
        @pl.when(cp < tiles - 6)
        def _():
            og_copy(cp + 6).start()

        @pl.when(cp == 0)
        def _():
            hear(2)

        og_copy(2 * cp).wait_recv()
        og_copy(2 * cp + 1).wait_recv()
        grad = og[:, wide(cp)].astype(F32)
        turned = (grad * g_all[:, wide(cp)].astype(F32)).astype(BF16)
        cg_all[0:rows, wide(cp)] = turned
        ch_copy(cp).start()
        gate_grad[0, :, wide(cp)] = (grad * conv[:, wide(cp)]).astype(BF16)
        for j in range(2):
            for b in range(blocks):
                own = turned[b * TILE:(b + 1) * TILE, j * TILE:(j + 1) * TILE]
                for g in range(per):
                    lhs_p[j, b, g * TILE:(g + 1) * TILE] = own * keeps[g]
        sums = []
        for j in range(2):
            products = []
            for b in range(blocks):
                window = v_all[b * TILE:(b + 2) * TILE, columns(2 * cp + j)]
                products.append(dot(lhs_p[j, b], window, ((1,), (1,))))
            skewed = []
            for g in range(per):
                acc = jnp.zeros((8, TILE), F32)
                for a in range(TILE // 8):
                    at = slice(a * 8, a * 8 + 8)
                    row = slice(g * TILE + a * 8, g * TILE + a * 8 + 8)
                    both = jnp.zeros((8, TILE), F32)
                    for b in range(blocks):
                        both = both + products[b][row, :TILE] * mask_q[b, at, :TILE]
                        both = both + products[b][row, TILE:] * mask_q[b, at, TILE:]
                    acc = acc + pltpu.roll(both, (TILE - 8 * a) % TILE, 1)
                skewed.append(acc)
            table = jnp.concatenate(skewed, axis=0)
            for bit in (1, 2, 4):
                table = jnp.where(sub & bit != 0, pltpu.roll(table, TILE - bit, 1), table)
            sums.append(jnp.sum(table.reshape(per, 8, TILE), axis=1))
        slots[cp, z] = jnp.concatenate(sums, axis=0)
        for k in range(1, n_z):
            z_copy(cp, k).start()
        return carry

    lax.fori_loop(0, tiles // 2, main_step, 0)

    def tail_step(cp, carry):
        value_step(cp)
        column_sum(cp)
        return carry

    lax.fori_loop(0, tiles // 2 - 1, tail_step, 0)
    value_step(tiles // 2 - 1)
    column_sum(tiles // 2 - 1)
    for cp in range(tiles // 2):
        pair_copy(cp).wait_recv()
    both = (mine[...] + theirs[...]).reshape(groups, TILE)
    filter_grad[0] = lax.dot_general(
        both, flip, (((1,), (0,)), ((), ())), precision=lax.Precision.HIGHEST, preferred_element_type=F32
    )

    def sent(ref, sem):
        pltpu.make_async_remote_copy(
            src_ref=ref, dst_ref=ref, send_sem=sem, recv_sem=vh_recv.at[0],
            device_id={"ctx": nxt}, device_id_type=MESH,
        ).wait_send()

    sent(v_all.at[pl.ds(0, TILE)], vh_send)
    sent(og, og_send)
    sent(cg_all.at[pl.ds(0, TILE)], ch_send)
    sent(slots.at[:, pl.ds(0, n_z - 1)], z_send)
    sent(mine, pair_send)


def hand_over(a, b, c, a_out, b_out, c_out, sems):
    parts = 4
    copies = [pltpu.make_async_copy(c, c_out, sems.at[2 * parts])]
    rows = a.shape[1] // parts
    for i in range(parts):
        at = pl.ds(i * rows, rows)
        copies.append(pltpu.make_async_copy(a.at[0, at], a_out.at[0, at], sems.at[i]))
        copies.append(pltpu.make_async_copy(b.at[0, at], b_out.at[0, at], sems.at[parts + i]))
    for copy in copies:
        copy.start()
    for copy in copies:
        copy.wait()


def solution(mesh):
    n_pipe, n_ctx = mesh.shape["pipe"], mesh.shape["ctx"]

    def body(values, gates, incoming, filters, lengths):
        _, rows, width = values.shape
        _, groups, taps = filters.shape
        tiles, blocks = width // TILE, rows // TILE
        chans = width // groups
        per = TILE // chans
        n_z = n_ctx // 2
        dma = pltpu.SemaphoreType.DMA
        any_spec = pl.BlockSpec(memory_space=pl.ANY)
        value_grad, gate_grad, filter_grad = pl.pallas_call(
            functools.partial(kernel, n_pipe, n_ctx, chans),
            out_shape=(
                pltpu.VMEM(values.shape, BF16),
                pltpu.VMEM(values.shape, BF16),
                pltpu.VMEM(filters.shape, F32),
            ),
            in_specs=[pl.BlockSpec(memory_space=pltpu.HBM)] * 5,
            out_specs=(pl.BlockSpec(memory_space=pltpu.VMEM),) * 3,
            scratch_shapes=[
                pltpu.VMEM((rows + TILE, width), BF16),
                pltpu.VMEM((rows, width), BF16),
                pltpu.VMEM((rows, width), BF16),
                pltpu.VMEM((rows + TILE, width), BF16),
                pltpu.VMEM((rows, width), F32),
                pltpu.VMEM((groups, taps), BF16),
                pltpu.SMEM(lengths.shape, jnp.int32),
                pltpu.VMEM((blocks, TILE, 2 * TILE), BF16),
                pltpu.VMEM((blocks, TILE, 2 * TILE), BF16),
                pltpu.VMEM((blocks, TILE, 2 * TILE), F32),
                pltpu.VMEM((tiles, per, taps), F32),
                pltpu.VMEM((tiles, per, taps), F32),
                pltpu.VMEM((per * TILE, 2 * TILE), BF16),
                pltpu.VMEM((per * TILE, 2 * TILE), BF16),
                pltpu.VMEM((tiles, per * TILE, 2 * TILE), BF16),
                pltpu.VMEM((tiles, blocks, per * TILE, 2 * TILE), BF16),
                pltpu.VMEM((2, blocks, per * TILE, TILE), BF16),
                pltpu.VMEM((tiles // 2, n_z, 2 * per, taps), F32),
                pltpu.VMEM((tiles // 2, 2 * per, taps), F32),
                pltpu.VMEM((tiles // 2, 2 * per, taps), F32),
                dma((4,)),
                dma, dma((tiles,)),
                dma, dma((tiles // 2,)),
                dma, dma((tiles // 2,)),
                dma, dma((tiles // 2,)),
                dma, dma((tiles // 2,)),
                pltpu.SemaphoreType.REGULAR((3,)),
            ],
            compiler_params=pltpu.CompilerParams(
                collective_id=0, has_side_effects=True, vmem_limit_bytes=62 * 1024 * 1024
            ),
            cost_estimate=pl.CostEstimate(
                flops=2 * 3 * groups * blocks * TILE * 2 * TILE * TILE,
                bytes_accessed=5 * rows * width * 2, transcendentals=0,
            ),
        )(values, gates, incoming, filters, lengths)
        results = (value_grad, gate_grad, filter_grad)
        return pl.pallas_call(
            hand_over,
            out_shape=tuple(jax.ShapeDtypeStruct(r.shape, r.dtype) for r in results),
            in_specs=[any_spec] * 3,
            out_specs=(any_spec,) * 3,
            scratch_shapes=[dma((9,))],
            compiler_params=pltpu.CompilerParams(vmem_limit_bytes=4 * 1024 * 1024),
        )(*results)

    shards = P("pipe", "ctx", "tp")
    taps = P("pipe", "tp", None)
    return jax.shard_map(
        body, mesh=mesh, in_specs=(shards, shards, shards, taps, P()), out_specs=(shards, shards, taps), check_vma=False
    )
```

time: 38.6 us -> 33 us (0.85)
  local copies, waits for them, and re-layouts: 3.34 us -> 0 us
  Pallas kernels: 34.5 us -> 32.3 us
    unnamed x7 -> x0, local copies, waits for them, and re-layouts: 3.34 us -> none
    pallas_call x1, Pallas kernels: 34.5 us -> 31.2 us  [body(): pl.pallas_call(functools.partial(kernel, n_pipe, n_ctx, chans), out_shape...]
    pallas_call x0 -> x1, Pallas kernels: none -> 1.05 us  [body(): pl.pallas_call(hand_over, out_shape=tuple((jax.ShapeDtypeStruct(r.shape,...]
where the time goes in v3:
time: 33 us; the launch traced here: 32.9 us
  Pallas kernels  32.3 us (98%)
  between operations  0.64 us (2%)
    pallas_call x1, Pallas kernels, body(): pl.pallas_call(functools.partial(kernel, n_pipe, n_ctx, chans), out_shape...  31.2 us
    pallas_call x1, Pallas kernels, body(): pl.pallas_call(hand_over, out_shape=tuple((jax.ShapeDtypeStruct(r.shape,...  1.05 us

profile of v3, /device:TPU:1, one launch (start us, length us, event | category | flops | bytes accessed | tf_op | source)
XLA Modules:
  0.0 32.9 jit_solution(13427149814872896762)
XLA Ops:
  0.6 31.2 %shard_map.76 = (bf16[1,256,1024]{2,1,0:T(8,128)(2,1)S(1)}, bf16[1,256,1024]{2,1,0:T(8,128)(2,1)S(1)}, f32[1,64,128]{2,1,0:T(8,128)S(1)}) custom-call(bf16[1,256,1024]{2,1,0:T(8,128)(2,1)} %values.1, bf16[1,256,1024]{2,1,0:T(8,128)(2,1)} %gates.1, bf16[1,256,1024]{2,1,0:T(8,128)(2,1)} %incoming.1, bf16[1,64,128]{2,1,0:T(8,128)(2,1)} %filters.1, s32[16]{0:T(128)} %lengths.1), custom_call_target="tpu_custom_call" | custom-call | flops 3221225472 | bytes 2621440 | tf_op jit(solution)/shard_map/pallas_call | solution.py:350
  31.8 1.0 %shard_map.77 = (bf16[1,256,1024]{2,1,0:T(8,128)(2,1)}, bf16[1,256,1024]{2,1,0:T(8,128)(2,1)}, f32[1,64,128]{2,1,0:T(8,128)}) custom-call(bf16[1,256,1024]{2,1,0:T(8,128)(2,1)S(1)} %get-tuple-element.6.a, bf16[1,256,1024]{2,1,0:T(8,128)(2,1)S(1)} %get-tuple-element.7.b, f32[1,64,128]{2,1,0:T(8,128)S(1)} %get-tuple-element.8.c), custom_call_target="tpu_custom_call" | custom-call | tf_op jit(solution)/shard_map/pallas_call | solution.py:397

commit v4 on v3

--- a/solution.py
+++ b/solution.py
@@ -105,8 +105,8 @@
             send_sem=vh_send, recv_sem=vh_recv.at[cp], device_id={"ctx": nxt}, device_id_type=MESH,
         )
 
+    og_copy(0).start()
     halo(0).start()
-    og_copy(0).start()
     tell(0)
     for cp in range(1, tiles // 2):
         halo(cp).start()
@@ -189,6 +189,10 @@
         return carry
 
     def first_step(cp, carry):
+        @pl.when(cp == 1)
+        def _():
+            og_copy(4).start()
+
         halo(cp).wait_recv()
         for j in range(2):
             convolve(2 * cp + j, 0, lhs_c.at[2 * cp + j])
@@ -199,7 +203,6 @@
     tables(tiles - 1, lhs_b)
     convolve(tiles - 2, 1, lhs_a)
     convolve(tiles - 1, 1, lhs_b)
-    og_copy(4).start()
     hear(1)
     lax.fori_loop(0, tiles // 2, first_step, 0)
     og_copy(5).start()
@@ -243,52 +246,67 @@
     sub = iota((per * 8, TILE), 0) % 8
     keeps = [(lane_group == g).astype(F32).astype(BF16) for g in range(per)]
 
+    def turn(at, cols):
+        grad = og[at, cols].astype(F32)
+        turned = (grad * g_all[at, cols].astype(F32)).astype(BF16)
+        cg_all[at, cols] = turned
+        return grad, turned
+
+    def outer(ct, b, own, lhs):
+        for g in range(per):
+            lhs[g * TILE:(g + 1) * TILE] = own * keeps[g]
+        window = v_all[b * TILE:(b + 2) * TILE, columns(ct)]
+        return dot(lhs[...], window, ((1,), (1,)))
+
+    def fold(products):
+        folded = []
+        for g in range(per):
+            acc = jnp.zeros((8, TILE), F32)
+            for a in range(TILE // 8):
+                at = slice(a * 8, a * 8 + 8)
+                row = slice(g * TILE + a * 8, g * TILE + a * 8 + 8)
+                both = jnp.zeros((8, TILE), F32)
+                for b, product in products:
+                    both = both + product[row, :TILE] * mask_q[b, at, :TILE]
+                    both = both + product[row, TILE:] * mask_q[b, at, TILE:]
+                acc = acc + pltpu.roll(both, (TILE - 8 * a) % TILE, 1)
+            folded.append(acc)
+        return jnp.concatenate(folded, axis=0)
+
+    def unskew(table):
+        for bit in (1, 2, 4):
+            table = jnp.where(sub & bit != 0, pltpu.roll(table, TILE - bit, 1), table)
+        return jnp.sum(table.reshape(per, 8, TILE), axis=1)
+
+    def share(cp, sums):
+        slots[cp, z] = jnp.concatenate(sums, axis=0)
+        for k in sorted(range(1, n_z), key=lambda k: -min(k, n_z - k)):
+            z_copy(cp, k).start()
+
     def main_step(cp, carry):
-        @pl.when(cp < tiles - 6)
-        def _():
-            og_copy(cp + 6).start()
-
         @pl.when(cp == 0)
         def _():
+            og_copy(6).start()
             hear(2)
+
+        @pl.when(cp == 1)
+        def _():
+            og_copy(7).start()
 
         og_copy(2 * cp).wait_recv()
         og_copy(2 * cp + 1).wait_recv()
-        grad = og[:, wide(cp)].astype(F32)
-        turned = (grad * g_all[:, wide(cp)].astype(F32)).astype(BF16)
-        cg_all[0:rows, wide(cp)] = turned
+
+        grad, turned = turn(slice(0, rows), wide(cp))
         ch_copy(cp).start()
         gate_grad[0, :, wide(cp)] = (grad * conv[:, wide(cp)]).astype(BF16)
-        for j in range(2):
-            for b in range(blocks):
-                own = turned[b * TILE:(b + 1) * TILE, j * TILE:(j + 1) * TILE]
-                for g in range(per):
-                    lhs_p[j, b, g * TILE:(g + 1) * TILE] = own * keeps[g]
         sums = []
         for j in range(2):
             products = []
             for b in range(blocks):
-                window = v_all[b * TILE:(b + 2) * TILE, columns(2 * cp + j)]
-                products.append(dot(lhs_p[j, b], window, ((1,), (1,))))
-            skewed = []
-            for g in range(per):
-                acc = jnp.zeros((8, TILE), F32)
-                for a in range(TILE // 8):
-                    at = slice(a * 8, a * 8 + 8)
-                    row = slice(g * TILE + a * 8, g * TILE + a * 8 + 8)
-                    both = jnp.zeros((8, TILE), F32)
-                    for b in range(blocks):
-                        both = both + products[b][row, :TILE] * mask_q[b, at, :TILE]
-                        both = both + products[b][row, TILE:] * mask_q[b, at, TILE:]
-                    acc = acc + pltpu.roll(both, (TILE - 8 * a) % TILE, 1)
-                skewed.append(acc)
-            table = jnp.concatenate(skewed, axis=0)
-            for bit in (1, 2, 4):
-                table = jnp.where(sub & bit != 0, pltpu.roll(table, TILE - bit, 1), table)
-            sums.append(jnp.sum(table.reshape(per, 8, TILE), axis=1))
-        slots[cp, z] = jnp.concatenate(sums, axis=0)
-        for k in range(1, n_z):
-            z_copy(cp, k).start()
+                own = turned[b * TILE:(b + 1) * TILE, j * TILE:(j + 1) * TILE]
+                products.append((b, outer(2 * cp + j, b, own, lhs_p.at[j, b])))
+            sums.append(unskew(fold(products)))
+        share(cp, sums)
         return carry
 
     lax.fori_loop(0, tiles // 2, main_step, 0)
@@ -303,10 +321,7 @@
     column_sum(tiles // 2 - 1)
     for cp in range(tiles // 2):
         pair_copy(cp).wait_recv()
-    both = (mine[...] + theirs[...]).reshape(groups, TILE)
-    filter_grad[0] = lax.dot_general(
-        both, flip, (((1,), (0,)), ((), ())), precision=lax.Precision.HIGHEST, preferred_element_type=F32
-    )
+    filter_grad[0] = (mine[...] + theirs[...]).reshape(groups, TILE)
 
     def sent(ref, sem):
         pltpu.make_async_remote_copy(
@@ -321,9 +336,9 @@
     sent(mine, pair_send)
 
 
-def hand_over(a, b, c, a_out, b_out, c_out, sems):
+def hand_over(a, b, c, a_out, b_out, c_out, flipped, sems):
     parts = 4
-    copies = [pltpu.make_async_copy(c, c_out, sems.at[2 * parts])]
+    copies = []
     rows = a.shape[1] // parts
     for i in range(parts):
         at = pl.ds(i * rows, rows)
@@ -331,6 +346,12 @@
         copies.append(pltpu.make_async_copy(b.at[0, at], b_out.at[0, at], sems.at[parts + i]))
     for copy in copies:
         copy.start()
+    flip = jnp.where(lax.rem(iota((TILE, TILE), 0) + iota((TILE, TILE), 1), TILE) == 0, 1.0, 0.0)
+    flipped[0] = lax.dot_general(
+        c[0], flip, (((1,), (0,)), ((), ())), precision=lax.Precision.HIGHEST, preferred_element_type=F32
+    )
+    copies.append(pltpu.make_async_copy(flipped, c_out, sems.at[2 * parts]))
+    copies[-1].start()
     for copy in copies:
         copy.wait()
 
@@ -397,9 +418,9 @@
         return pl.pallas_call(
             hand_over,
             out_shape=tuple(jax.ShapeDtypeStruct(r.shape, r.dtype) for r in results),
-            in_specs=[any_spec] * 3,
+            in_specs=[any_spec, any_spec, pl.BlockSpec(memory_space=pltpu.VMEM)],
             out_specs=(any_spec,) * 3,
-            scratch_shapes=[dma((9,))],
+            scratch_shapes=[pltpu.VMEM(filters.shape, F32), dma((9,))],
             compiler_params=pltpu.CompilerParams(vmem_limit_bytes=4 * 1024 * 1024),
         )(*results)
 

time: 33 us -> 32.7 us (level)
  Pallas kernels: 32.3 us -> 31.9 us
where the time goes in v4:
time: 32.7 us; the launch traced here: 32.6 us
  Pallas kernels  31.9 us (98%)
  between operations  0.64 us (2%)
    pallas_call x1, Pallas kernels, body(): pl.pallas_call(functools.partial(kernel, n_pipe, n_ctx, chans), out_shape...  30.9 us
    pallas_call x1, Pallas kernels, body(): pl.pallas_call(hand_over, out_shape=tuple((jax.ShapeDtypeStruct(r.shape,...  1.04 us

profile of v4, /device:TPU:1, one launch (start us, length us, event | category | flops | bytes accessed | tf_op | source)
XLA Modules:
  0.0 32.6 jit_solution(6299458118439818481)
XLA Ops:
  0.6 30.9 %shard_map.76 = (bf16[1,256,1024]{2,1,0:T(8,128)(2,1)S(1)}, bf16[1,256,1024]{2,1,0:T(8,128)(2,1)S(1)}, f32[1,64,128]{2,1,0:T(8,128)S(1)}) custom-call(bf16[1,256,1024]{2,1,0:T(8,128)(2,1)} %values.1, bf16[1,256,1024]{2,1,0:T(8,128)(2,1)} %gates.1, bf16[1,256,1024]{2,1,0:T(8,128)(2,1)} %incoming.1, bf16[1,64,128]{2,1,0:T(8,128)(2,1)} %filters.1, s32[16]{0:T(128)} %lengths.1), custom_call_target="tpu_custom_call" | custom-call | flops 3221225472 | bytes 2621440 | tf_op jit(solution)/shard_map/pallas_call | solution.py:371
  31.5 1.0 %shard_map.77 = (bf16[1,256,1024]{2,1,0:T(8,128)(2,1)}, bf16[1,256,1024]{2,1,0:T(8,128)(2,1)}, f32[1,64,128]{2,1,0:T(8,128)}) custom-call(bf16[1,256,1024]{2,1,0:T(8,128)(2,1)S(1)} %get-tuple-element.6.a, bf16[1,256,1024]{2,1,0:T(8,128)(2,1)S(1)} %get-tuple-element.7.b, f32[1,64,128]{2,1,0:T(8,128)S(1)} %get-tuple-element.8.c), custom_call_target="tpu_custom_call" | custom-call | tf_op jit(solution)/shard_map/pallas_call | solution.py:418

commit v5 on v4

--- a/solution.py
+++ b/solution.py
@@ -60,12 +60,11 @@
         load.start()
 
     barrier = pltpu.get_barrier_semaphore()
-    pl.semaphore_signal(barrier, inc=1, device_id={"pipe": pipe_prev}, device_id_type=MESH)
     pl.semaphore_signal(barrier, inc=1, device_id={"pipe": pipe_next}, device_id_type=MESH)
 
     pl.semaphore_signal(barrier, inc=1, device_id={"ctx": prev}, device_id_type=MESH)
     pl.semaphore_signal(barrier, inc=1, device_id={"ctx": nxt}, device_id_type=MESH)
-    pl.semaphore_wait(barrier, 4)
+    pl.semaphore_wait(barrier, 3)
 
     rounds = (n_ctx // 2).bit_length() - 1
 

time: 32.7 us -> 32.3 us (0.988)
  Pallas kernels: 31.9 us -> 31.5 us
    pallas_call x1, Pallas kernels: 30.9 us -> 30.5 us  [body(): pl.pallas_call(functools.partial(kernel, n_pipe, n_ctx, chans), out_shape...]
where the time goes in v5:
time: 32.3 us; the launch traced here: 32.2 us
  Pallas kernels  31.5 us (98%)
  between operations  0.64 us (2%)
    pallas_call x1, Pallas kernels, body(): pl.pallas_call(functools.partial(kernel, n_pipe, n_ctx, chans), out_shape...  30.5 us
    pallas_call x1, Pallas kernels, body(): pl.pallas_call(hand_over, out_shape=tuple((jax.ShapeDtypeStruct(r.shape,...  1.04 us

profile of v5, /device:TPU:1, one launch (start us, length us, event | category | flops | bytes accessed | tf_op | source)
XLA Modules:
  0.0 32.2 jit_solution(5717518800536931407)
XLA Ops:
  0.6 30.5 %shard_map.76 = (bf16[1,256,1024]{2,1,0:T(8,128)(2,1)S(1)}, bf16[1,256,1024]{2,1,0:T(8,128)(2,1)S(1)}, f32[1,64,128]{2,1,0:T(8,128)S(1)}) custom-call(bf16[1,256,1024]{2,1,0:T(8,128)(2,1)} %values.1, bf16[1,256,1024]{2,1,0:T(8,128)(2,1)} %gates.1, bf16[1,256,1024]{2,1,0:T(8,128)(2,1)} %incoming.1, bf16[1,64,128]{2,1,0:T(8,128)(2,1)} %filters.1, s32[16]{0:T(128)} %lengths.1), custom_call_target="tpu_custom_call" | custom-call | flops 3221225472 | bytes 2621440 | tf_op jit(solution)/shard_map/pallas_call | solution.py:370
  31.1 1.0 %shard_map.77 = (bf16[1,256,1024]{2,1,0:T(8,128)(2,1)}, bf16[1,256,1024]{2,1,0:T(8,128)(2,1)}, f32[1,64,128]{2,1,0:T(8,128)}) custom-call(bf16[1,256,1024]{2,1,0:T(8,128)(2,1)S(1)} %get-tuple-element.6.a, bf16[1,256,1024]{2,1,0:T(8,128)(2,1)S(1)} %get-tuple-element.7.b, f32[1,64,128]{2,1,0:T(8,128)S(1)} %get-tuple-element.8.c), custom_call_target="tpu_custom_call" | custom-call | tf_op jit(solution)/shard_map/pallas_call | solution.py:417
